TPU v7x, 32 devices: a whole 2x2x4 slice. The times are simulated.
32 devices in a mesh: dp: 8 (over z, core), ctx: 4 (over y, x).
Axes of the slice: x: 2, y: 2, z: 4, core: 2. Of those that a mesh axis runs over, the one named last changes fastest.
Arguments:
- queries: bfloat16 [8, 512, 4096], P('dp', 'ctx'), may hold values from -8 to 8
- key_rows: bfloat16 [8, 512, 512], P('dp', 'ctx'), may hold values from -8 to 8
- values: bfloat16 [8, 512, 512], P('dp', 'ctx'), may hold values from -6 to 6
- outputs: bfloat16 [8, 512, 4096], P('dp', 'ctx'), may hold values from -4 to 4
- out_grads: bfloat16 [8, 512, 4096], P('dp', 'ctx'), may hold values from -6 to 6
- depths: int32 [8, 512], P('dp', 'ctx'), may hold values from 0 to 63, as said below
- subtree_end: int32 [8, 512], P('dp', 'ctx'), may hold values from 64 to 512, as said below
- file_lengths: int32 [8, 8], P('dp'), may hold values from 1 to 384, 512 in all within a row
- slopes: float32 [32], replicated, may hold values from 0.02 to 0.5
- ancestor_gain: float32 [32], replicated, may hold values from 0.5 to 3
Outputs:
- query_grads: bfloat16 [8, 512, 4096], P('dp', 'ctx')
- key_grads: bfloat16 [8, 512, 512], P('dp', 'ctx')
- value_grads: bfloat16 [8, 512, 512], P('dp', 'ctx')
- bias_grads: float32 [32, 2], P('ctx')
Inputs may be any that keep to these rules, and one draw needn't show every extreme that they name: `depths`: token t has depth t for t < 64; afterwards the depth changes by at most one from a token to the next. `subtree_end`: the first later position of the same sequence whose depth is not above the token's depth, or 512 where there is none.
All inputs are finite; a program needn't handle non-finite values.
Results may differ from a plain program's by a relative error of at most 0.012.
Values may be sent and summed in bfloat16 or wider, within the bound.
No kernel may reach another device: no remote copies, remote signals or barrier semaphores. Data moves between devices by JAX's collectives and lax.ppermute only.
A program may use at most 64 MiB of HBM per device.

v0:
```python
import functools

import jax
import jax.numpy as jnp
from jax import lax
from jax.experimental import pallas as pl
from jax.experimental.pallas import tpu as pltpu
from jax.sharding import PartitionSpec as P

WIDTH = 128
LOG2E = 1.4426950408889634
MASKED = -1e30
META_ROWS = 16
END_UNIT = 64
CHUNKS = 2

VMEM_LIMIT = 32 * 1024 * 1024


def dot_nt(a, b):
    return lax.dot_general(a, b, (((1,), (1,)), ((), ())), preferred_element_type=jnp.float32)


def dot_nn(a, b):
    return lax.dot_general(a, b, (((1,), (0,)), ((), ())), preferred_element_type=jnp.float32)


def pack_kernel(key_ref, value_ref, depth_ref, end_ref, *message_refs):
    tokens = key_ref.shape[0]
    groups = key_ref.shape[1] // WIDTH // len(message_refs)
    for chunk, message_ref in enumerate(message_refs):
        for group in range(groups):
            source = slice((chunk * groups + group) * WIDTH, (chunk * groups + group + 1) * WIDTH)
            at = 2 * group * WIDTH
            message_ref[0:tokens, at : at + WIDTH] = key_ref[:, source]
            message_ref[0:tokens, at + WIDTH : at + 2 * WIDTH] = value_ref[:, source]
    depth = depth_ref[...]
    end = end_ref[...]
    end_high = end // END_UNIT
    end_low = end - end_high * END_UNIT
    row = lax.broadcasted_iota(jnp.int32, (META_ROWS, tokens), 0)
    meta = jnp.where(row == 0, depth, jnp.where(row == 1, end_high, end_low))
    meta = meta.astype(jnp.float32).astype(jnp.bfloat16)
    below = slice(tokens, tokens + META_ROWS)
    message_refs[0][below, 0:tokens] = meta
    message_refs[0][below, tokens:] = jnp.zeros(
        (META_ROWS, 2 * groups * WIDTH - tokens), jnp.bfloat16
    )


def as_column(row):
    size = row.shape[1]
    return jnp.transpose(jnp.broadcast_to(row, (size, size)))


def fold_rows(block):
    return jnp.sum(block.reshape(block.shape[0] // 8, 8, block.shape[1]), axis=0)


def main_kernel(
    blocks,
    heads_per_group,
    unroll_pairs,
    first_group,
    lengths_ref,
    slope_ref,
    gain_ref,
    depth_ref,
    end_ref,
    query_ref,
    output_ref,
    grad_ref,
    key_ref,
    value_ref,
    *refs,
):
    tokens = query_ref.shape[0]
    remote = refs[0 : blocks - 1]
    remote_meta = refs[blocks - 1 : 2 * (blocks - 1)]
    rest = refs[2 * (blocks - 1) :]
    if first_group:
        bias_before = rest[0]
        rest = rest[2 + blocks :]
    query_grad_ref = rest[0]
    part_refs = rest[1 : 1 + blocks]
    bias_ref = rest[1 + blocks]
    (
        distance_ref,
        ancestor_ref,
        slope_rows,
        gain_rows,
        key_acc,
        value_acc,
        weight_ref,
        probs_ref,
        dscore_ref,
    ) = rest[2 + blocks :]
    group = pl.program_id(0)
    factor = WIDTH**-0.5

    @pl.when(group == 0)
    def _():
        here = lax.axis_index("ctx")
        query_pos = here * tokens + lax.broadcasted_iota(jnp.int32, (tokens, tokens), 1)
        start = jnp.zeros((tokens, tokens), jnp.int32)
        bound = jnp.int32(0)
        for index in range(lengths_ref.shape[1]):
            bound = bound + lengths_ref[0, index]
            start = jnp.where(query_pos >= bound, bound, start)
        query_depth = jnp.broadcast_to(depth_ref[...].astype(jnp.float32), (tokens, tokens))
        for shift in range(blocks):
            key_pos = (here - shift) * tokens + lax.broadcasted_iota(
                jnp.int32, (tokens, tokens), 0
            )
            if shift == 0:
                key_depth = as_column(depth_ref[...].astype(jnp.float32))
                key_end = as_column(end_ref[...].astype(jnp.float32))
            else:
                meta = remote_meta[shift - 1][...].astype(jnp.float32)
                key_depth = as_column(meta[0:1])
                key_end = as_column(meta[1:2] * END_UNIT + meta[2:3])
            inside = query_pos.astype(jnp.float32) < key_end
            allowed = (key_pos <= query_pos) & (key_pos >= start) & (key_pos >= 0)
            rows = slice(shift * tokens, (shift + 1) * tokens)
            distance_ref[rows, :] = jnp.abs(query_depth - key_depth)
            ancestor_ref[rows, :] = jnp.where(allowed, jnp.where(inside, 1.0, 0.0), MASKED)

    keys = jnp.concatenate([key_ref[...]] + [r[:, 0:WIDTH] for r in remote], axis=0)
    values = jnp.concatenate([value_ref[...]] + [r[:, WIDTH:] for r in remote], axis=0)
    value_ext = jnp.concatenate([values, jnp.full(values.shape, -1.0, jnp.bfloat16)], axis=1)
    keys_across = jnp.transpose(keys)
    block_rows = [slice(shift * tokens, (shift + 1) * tokens) for shift in range(blocks)]

    def head_columns(ref, pair):
        parts = []
        for half in range(2):
            at = (2 * pair + half) * WIDTH
            if not isinstance(pair, int):
                at = pl.multiple_of(at, WIDTH)
            parts.append(ref[:, pl.ds(at, WIDTH)])
        return jnp.concatenate(parts, axis=0)

    def scores(pair, slot):
        query_pair = head_columns(query_ref, pair)
        grad_pair = head_columns(grad_ref, pair)
        output_pair = head_columns(output_ref, pair)
        grad_ext = jnp.concatenate([grad_pair, grad_pair * output_pair], axis=1)
        raw = dot_nt(keys, query_pair)
        scales = []
        for half in range(2):
            head = (first_group + group) * heads_per_group + 2 * pair + half
            gain = gain_ref[head] * LOG2E
            slope = slope_ref[head] * LOG2E
            lanes = slice(half * tokens, (half + 1) * tokens)
            tops, totals = [], []
            for rows in block_rows:
                score = raw[rows, lanes] * (factor * LOG2E) + (
                    gain * ancestor_ref[rows, :] - slope * distance_ref[rows, :]
                )
                top = jnp.max(score, axis=0, keepdims=True)
                weight = jnp.exp2(score - top)
                weight_ref[slot, rows, lanes] = weight
                tops.append(top)
                totals.append(jnp.sum(weight, axis=0, keepdims=True))
            top = functools.reduce(jnp.maximum, tops)
            shrink = [jnp.exp2(t - top) for t in tops]
            total = sum(a * b for a, b in zip(totals, shrink))
            inverse = 1.0 / total
            scales.append([s * inverse for s in shrink])
        centred = dot_nt(value_ext, grad_ext)
        for half in range(2):
            head = (first_group + group) * heads_per_group + 2 * pair + half
            lanes = slice(half * tokens, (half + 1) * tokens)
            slope_sum, gain_sum = 0.0, 0.0
            for rows, scale in zip(block_rows, scales[half]):
                probs = weight_ref[slot, rows, lanes] * scale
                dscore = probs * centred[rows, lanes]
                probs_ref[slot, rows, lanes] = probs.astype(jnp.bfloat16)
                dscore_ref[slot, rows, lanes] = dscore.astype(jnp.bfloat16)
                slope_sum = slope_sum + fold_rows(dscore * distance_ref[rows, :])
                gain_sum = gain_sum + fold_rows(dscore * ancestor_ref[rows, :])
            at = pl.ds(group * heads_per_group + 2 * pair + half, 1)
            slope_rows[at, :] = -jnp.sum(slope_sum, axis=0, keepdims=True)
            gain_rows[at, :] = jnp.sum(gain_sum, axis=0, keepdims=True)

    def gradients(pair, slot, first):
        query_pair = head_columns(query_ref, pair)
        grad_pair = head_columns(grad_ref, pair)
        dscore_b = dscore_ref[slot]
        key_part = dot_nn(dscore_b, query_pair)
        value_part = dot_nn(probs_ref[slot], grad_pair)
        if first:
            key_acc[...] = key_part
            value_acc[...] = value_part
        else:
            key_acc[...] += key_part
            value_acc[...] += value_part
        query_across = dot_nn(keys_across, dscore_b) * factor
        query_pair_grad = jnp.transpose(query_across).astype(jnp.bfloat16)
        for half in range(2):
            at = (2 * pair + half) * WIDTH
            if not isinstance(pair, int):
                at = pl.multiple_of(at, WIDTH)
            query_grad_ref[:, pl.ds(at, WIDTH)] = query_pair_grad[
                half * tokens : (half + 1) * tokens
            ]

    pairs = heads_per_group // 2
    if unroll_pairs:
        scores(0, 0)
        for pair in range(1, pairs):
            scores(pair, pair % 2)
            gradients(pair - 1, (pair - 1) % 2, pair == 1)
        gradients(pairs - 1, (pairs - 1) % 2, pairs == 1)
    else:
        key_acc[...] = jnp.zeros_like(key_acc)
        value_acc[...] = jnp.zeros_like(value_acc)

        @pl.loop(0, pairs)
        def _(pair):
            scores(pair, 0)
            gradients(pair, 0, False)

    for shift in range(blocks):
        rows = block_rows[shift]
        part_refs[shift][:, 0:WIDTH] = (key_acc[rows, :] * factor).astype(jnp.bfloat16)
        part_refs[shift][:, WIDTH:] = value_acc[rows, :].astype(jnp.bfloat16)

    @pl.when(group == pl.num_programs(0) - 1)
    def _():
        slope_sum = jnp.sum(slope_rows[...], axis=1, keepdims=True)
        gain_sum = jnp.sum(gain_rows[...], axis=1, keepdims=True)
        shape = slope_rows.shape
        lane = lax.broadcasted_iota(jnp.int32, shape, 1)
        row = lax.broadcasted_iota(jnp.int32, shape, 0)
        local = bias_ref.shape[3]
        for part in range(bias_ref.shape[1]):
            mine = lane == row - part * local + first_group * heads_per_group
            mine = mine & (lane < local) & (lane >= 0)
            for kind, column in ((0, slope_sum), (1, gain_sum)):
                line = jnp.sum(jnp.where(mine, column, 0.0), axis=0, keepdims=True)
                line = line[None, :, 0:local]
                if first_group:
                    line = line + bias_before[0:1, part, kind : kind + 1, :]
                bias_ref[:, part, kind : kind + 1, :] = jnp.broadcast_to(
                    line, (bias_ref.shape[0], 1, local)
                )


def final_kernel(blocks, *refs):
    parts = refs[0:blocks]
    bias_parts, key_out, value_out, bias_out = refs[blocks:]
    for group in range(key_out.shape[1] // WIDTH):
        to = slice(group * WIDTH, (group + 1) * WIDTH)
        for kind, out in enumerate((key_out, value_out)):
            at = (2 * group + kind) * WIDTH
            total = parts[0][:, at : at + WIDTH].astype(jnp.float32)
            for shift in range(1, blocks):
                total = total + parts[shift][:, at : at + WIDTH].astype(jnp.float32)
            out[:, to] = total.astype(jnp.bfloat16)
    bias_out[...] = jnp.sum(bias_parts[...], axis=0)


def body(
    queries,
    key_rows,
    values,
    outputs,
    out_grads,
    depths,
    subtree_end,
    file_lengths,
    slopes,
    ancestor_gain,
):
    blocks = lax.axis_size("ctx")
    replicas = lax.axis_size("dp")
    tokens, width_all = queries.shape[1:]
    kv_width = key_rows.shape[2]
    heads_all = width_all // WIDTH
    kv_heads = kv_width // WIDTH
    heads_per_group = heads_all // kv_heads
    group_columns = heads_per_group * WIDTH
    local_heads = heads_all // blocks
    keys_seen = blocks * tokens
    chunk_groups = kv_heads // CHUNKS
    bf16, f32 = jnp.bfloat16, jnp.float32
    vmem = pl.BlockSpec(memory_space=pltpu.VMEM)
    smem = pl.BlockSpec(memory_space=pltpu.SMEM)
    anywhere = pl.BlockSpec(memory_space=pl.ANY)
    params = pltpu.CompilerParams(vmem_limit_bytes=VMEM_LIMIT)

    messages = pl.pallas_call(
        pack_kernel,
        out_shape=[
            jax.ShapeDtypeStruct(
                (tokens + (META_ROWS if chunk == 0 else 0), 2 * chunk_groups * WIDTH), bf16
            )
            for chunk in range(CHUNKS)
        ],
        in_specs=[vmem] * 4,
        out_specs=[vmem] * CHUNKS,
        compiler_params=params,
        name="pack",
    )(key_rows[0], values[0], depths, subtree_end)
    arrived = [
        [
            lax.ppermute(message, "ctx", [(i, i + shift) for i in range(blocks - shift)])
            for shift in range(1, blocks)
        ]
        for message in messages
    ]

    bias_shape = (replicas, blocks, 2, local_heads)
    matmul_flops = 2 * tokens * keys_seen * WIDTH * heads_all
    out_shape = (
        [jax.ShapeDtypeStruct((tokens, width_all), bf16)]
        + [jax.ShapeDtypeStruct((tokens, 2 * kv_width), bf16)] * blocks
        + [jax.ShapeDtypeStruct(bias_shape, f32)]
    )
    results = None
    for chunk in range(CHUNKS):
        first = chunk * chunk_groups
        wide = pl.BlockSpec((tokens, group_columns), lambda g, first=first: (0, first + g))
        own_spec = pl.BlockSpec((tokens, WIDTH), lambda g, first=first: (0, first + g))
        remote_spec = pl.BlockSpec((tokens, 2 * WIDTH), lambda g: (0, g))
        part_spec = pl.BlockSpec((tokens, 2 * WIDTH), lambda g, first=first: (0, first + g))
        meta_spec = pl.BlockSpec((META_ROWS, tokens), lambda g: (tokens // META_ROWS, 0))
        row_spec = pl.BlockSpec((1, tokens), lambda g: (0, 0))
        bias_spec = pl.BlockSpec(bias_shape, lambda g: (0, 0, 0, 0))
        operands = [
            file_lengths,
            slopes,
            ancestor_gain,
            depths,
            subtree_end,
            queries[0],
            outputs[0],
            out_grads[0],
            key_rows[0],
            values[0],
            *arrived[chunk],
            *arrived[0],
        ]
        specs = [smem, smem, smem, row_spec, row_spec, wide, wide, wide, own_spec, own_spec]
        specs = specs + [remote_spec] * (blocks - 1) + [meta_spec] * (blocks - 1)
        aliases = {}
        if chunk:
            operands = operands + [results[1 + blocks]] + list(results[0 : 1 + blocks])
            specs = specs + [bias_spec] + [anywhere] * (1 + blocks)
            aliases = {len(operands) - 1 - blocks + i: i for i in range(1 + blocks)}
        results = pl.pallas_call(
            functools.partial(main_kernel, blocks, heads_per_group, blocks <= 4, first),
            grid=(chunk_groups,),
            out_shape=out_shape,
            in_specs=specs,
            out_specs=[wide] + [part_spec] * blocks + [bias_spec],
            scratch_shapes=[
                pltpu.VMEM((keys_seen, tokens), f32),
                pltpu.VMEM((keys_seen, tokens), f32),
                pltpu.VMEM((chunk_groups * heads_per_group, tokens), f32),
                pltpu.VMEM((chunk_groups * heads_per_group, tokens), f32),
                pltpu.VMEM((keys_seen, WIDTH), f32),
                pltpu.VMEM((keys_seen, WIDTH), f32),
                pltpu.VMEM((2, keys_seen, 2 * tokens), f32),
                pltpu.VMEM((2, keys_seen, 2 * tokens), bf16),
                pltpu.VMEM((2, keys_seen, 2 * tokens), bf16),
            ],
            input_output_aliases=aliases,
            compiler_params=params,
            cost_estimate=pl.CostEstimate(
                flops=5 * matmul_flops // CHUNKS,
                bytes_accessed=10 * tokens * width_all // CHUNKS,
                transcendentals=tokens * keys_seen * heads_all // CHUNKS,
            ),
            name=f"attend_{chunk}",
        )(*operands)
    query_grads = results[0]
    parts = list(results[1 : 1 + blocks])
    bias_parts = results[1 + blocks].reshape(replicas * blocks, 2, local_heads)
    for shift in range(1, blocks):
        back = [(i + shift, i) for i in range(blocks - shift)]
        parts[shift] = lax.ppermute(parts[shift], "ctx", back)
    bias_parts = lax.all_to_all(bias_parts, ("dp", "ctx"), split_axis=0, concat_axis=0, tiled=True)

    key_grads, value_grads, bias_grads = pl.pallas_call(
        functools.partial(final_kernel, blocks),
        out_shape=[
            jax.ShapeDtypeStruct((tokens, kv_width), bf16),
            jax.ShapeDtypeStruct((tokens, kv_width), bf16),
            jax.ShapeDtypeStruct((2, local_heads), f32),
        ],
        in_specs=[vmem] * (blocks + 1),
        out_specs=[vmem] * 3,
        compiler_params=params,
        name="combine",
    )(*parts, bias_parts)
    return (query_grads[None], key_grads[None], value_grads[None], bias_grads.T)


def solution(mesh):
    in_specs = (
        P("dp", "ctx", None),
        P("dp", "ctx", None),
        P("dp", "ctx", None),
        P("dp", "ctx", None),
        P("dp", "ctx", None),
        P("dp", "ctx"),
        P("dp", "ctx"),
        P("dp", None),
        P(),
        P(),
    )
    out_specs = (P("dp", "ctx", None), P("dp", "ctx", None), P("dp", "ctx", None), P("ctx", None))
    return jax.shard_map(body, mesh=mesh, in_specs=in_specs, out_specs=out_specs, check_vma=False)
```

profile of v0, /device:TPU:0, one launch (start us, length us, event | category | flops | bytes accessed | tf_op | source)
XLA Modules:
  0.0 57.3 jit_solution(16634986779666531000)
XLA Ops:
  0.7 0.6 %copy-done.5 = s32[1,128]{1,0:T(1,128)S(1)} copy-done((s32[1,128]{1,0:T(1,128)S(1)}, s32[1,128]{1,0:T(1,128)}, u32[]{:S(2)}) %copy-start.5) | copy-done | bytes 536
  1.3 0.0 copy-done.6
  1.3 0.9 %copy-done.3 = bf16[1,128,512]{2,1,0:T(8,128)(2,1)S(1)} copy-done((bf16[1,128,512]{2,1,0:T(8,128)(2,1)S(1)}, bf16[1,128,512]{2,1,0:T(8,128)(2,1)}, u32[]{:S(2)}) %copy-start.3) | copy-done | bytes 131096
  2.2 0.9 %copy-done.4 = bf16[1,128,512]{2,1,0:T(8,128)(2,1)S(1)} copy-done((bf16[1,128,512]{2,1,0:T(8,128)(2,1)S(1)}, bf16[1,128,512]{2,1,0:T(8,128)(2,1)}, u32[]{:S(2)}) %copy-start.4) | copy-done | bytes 131096
  3.1 0.1 pack.1
  3.2 5.8 %collective-permute-start.5 = (bf16[144,512]{1,0:T(8,128)(2,1)S(1)}, bf16[144,512]{1,0:T(8,128)(2,1)S(1)}, u32[]{:S(2)}, u32[]{:S(2)}) collective-permute-start(bf16[144,512]{1,0:T(8,128)(2,1)S(1)} %get-tuple-element.22), channel_id=1, source_target_pairs={{0,3},{4,7},{8,11},{12,15},{16,19},{20,23},{24,27},{28,31}} | collective-permute-start | bytes 442376 | tf_op jit(solution)/shard_map/ppermute | solution.py:308
  9.0 1.3 %collective-permute-start.4 = (bf16[144,512]{1,0:T(8,128)(2,1)S(1)}, bf16[144,512]{1,0:T(8,128)(2,1)S(1)}, u32[]{:S(2)}, u32[]{:S(2)}) collective-permute-start(bf16[144,512]{1,0:T(8,128)(2,1)S(1)} %get-tuple-element.22), channel_id=1, source_target_pairs={{0,2},{1,3},{4,6},{5,7},{8,10},{9,11},{12,14},{13,15},{16,18},{17,... | collective-permute-start | bytes 442376 | tf_op jit(solution)/shard_map/ppermute | solution.py:308
  10.3 2.5 %collective-permute-start.3 = (bf16[144,512]{1,0:T(8,128)(2,1)S(1)}, bf16[144,512]{1,0:T(8,128)(2,1)S(1)}, u32[]{:S(2)}, u32[]{:S(2)}) collective-permute-start(bf16[144,512]{1,0:T(8,128)(2,1)S(1)} %get-tuple-element.22), channel_id=1, source_target_pairs={{0,1},{1,2},{2,3},{4,5},{5,6},{6,7},{8,9},{9,10},{10,11},{12,13},{... | collective-permute-start | bytes 442376 | tf_op jit(solution)/shard_map/ppermute | solution.py:308
  12.8 1.3 %collective-permute-start.2 = (bf16[128,512]{1,0:T(8,128)(2,1)S(1)}, bf16[128,512]{1,0:T(8,128)(2,1)S(1)}, u32[]{:S(2)}, u32[]{:S(2)}) collective-permute-start(bf16[128,512]{1,0:T(8,128)(2,1)S(1)} %get-tuple-element.21), channel_id=1, source_target_pairs={{0,3},{4,7},{8,11},{12,15},{16,19},{20,23},{24,27},{28,31}} | collective-permute-start | bytes 393224 | tf_op jit(solution)/shard_map/ppermute | solution.py:308
  14.1 1.3 %collective-permute-start.1 = (bf16[128,512]{1,0:T(8,128)(2,1)S(1)}, bf16[128,512]{1,0:T(8,128)(2,1)S(1)}, u32[]{:S(2)}, u32[]{:S(2)}) collective-permute-start(bf16[128,512]{1,0:T(8,128)(2,1)S(1)} %get-tuple-element.21), channel_id=1, source_target_pairs={{0,2},{1,3},{4,6},{5,7},{8,10},{9,11},{12,14},{13,15},{16,18},{17,... | collective-permute-start | bytes 393224 | tf_op jit(solution)/shard_map/ppermute | solution.py:308
  15.4 1.3 %collective-permute-start = (bf16[128,512]{1,0:T(8,128)(2,1)S(1)}, bf16[128,512]{1,0:T(8,128)(2,1)S(1)}, u32[]{:S(2)}, u32[]{:S(2)}) collective-permute-start(bf16[128,512]{1,0:T(8,128)(2,1)S(1)} %get-tuple-element.21), channel_id=1, source_target_pairs={{0,1},{1,2},{2,3},{4,5},{5,6},{6,7},{8,9},{9,10},{10,11},{12,13},{... | collective-permute-start | bytes 393224 | tf_op jit(solution)/shard_map/ppermute | solution.py:308
  16.7 3.7 %collective-permute-done.4.refs_1_.refs_4_ = bf16[144,512]{1,0:T(8,128)(2,1)S(1)} collective-permute-done((bf16[144,512]{1,0:T(8,128)(2,1)S(1)}, bf16[144,512]{1,0:T(8,128)(2,1)S(1)}, u32[]{:S(2)}, u32[]{:S(2)}) %collective-permute-start.4) | collective-permute-done | bytes 147488 | tf_op jit(solution)/shard_map/ppermute | solution.py:308
  20.4 0.6 %copy-done.7 = s32[1,8]{1,0:T(1,128)S(1)} copy-done((s32[1,8]{1,0:T(1,128)S(1)}, s32[1,8]{1,0:T(1,128)}, u32[]{:S(2)}) %copy-start.7) | copy-done | bytes 56
  21.1 0.0 copy-done.9
  21.1 1.2 %copy-done = bf16[1,128,4096]{2,1,0:T(8,128)(2,1)S(1)} copy-done((bf16[1,128,4096]{2,1,0:T(8,128)(2,1)S(1)}, bf16[1,128,4096]{2,1,0:T(8,128)(2,1)}, u32[]{:S(2)}) %copy-start) | copy-done | bytes 1048600
  22.3 1.2 %copy-done.1 = bf16[1,128,4096]{2,1,0:T(8,128)(2,1)S(1)} copy-done((bf16[1,128,4096]{2,1,0:T(8,128)(2,1)S(1)}, bf16[1,128,4096]{2,1,0:T(8,128)(2,1)}, u32[]{:S(2)}) %copy-start.1) | copy-done | bytes 1048600
  23.6 1.2 %copy-done.2 = bf16[1,128,4096]{2,1,0:T(8,128)(2,1)S(1)} copy-done((bf16[1,128,4096]{2,1,0:T(8,128)(2,1)S(1)}, bf16[1,128,4096]{2,1,0:T(8,128)(2,1)}, u32[]{:S(2)}) %copy-start.2) | copy-done | bytes 1048600
  24.8 6.2 %attend_0.1 = (bf16[128,4096]{1,0:T(8,128)(2,1)}, bf16[128,1024]{1,0:T(8,128)(2,1)S(1)}, bf16[128,1024]{1,0:T(8,128)(2,1)S(1)}, bf16[128,1024]{1,0:T(8,128)(2,1)...) custom-call(s32[1,8]{1,0:T(1,128)S(1)} %copy-done.7, f32[32]{0:T(128)S(1)} %copy-done.8, ...), custom_call_target="tpu_custom_call" | custom-call | flops 1342177280 | bytes 2621440 | tf_op jit(solution)/shard_map/attend_0/pallas_call | solution.py:352
  31.0 6.3 %attend_1.1 = (bf16[128,4096]{1,0:T(8,128)(2,1)}, bf16[128,1024]{1,0:T(8,128)(2,1)S(1)}, bf16[128,1024]{1,0:T(8,128)(2,1)S(1)}, bf16[128,1024]{1,0:T(8,128)(2,1)...) custom-call(s32[1,8]{1,0:T(1,128)S(1)} %copy-done.7, ...), custom_call_target="tpu_custom_call", output_to_operand_aliasing={{0}: (17, {}), {1}: (18, {}), {2}: (19, {}), {3}: (20, {}),... | custom-call | flops 1342177280 | bytes 2621440 | tf_op jit(solution)/shard_map/attend_1/pallas_call | solution.py:352
  37.3 1.3 %collective-permute-start.6 = (bf16[128,1024]{1,0:T(8,128)(2,1)S(1)}, bf16[128,1024]{1,0:T(8,128)(2,1)S(1)}, u32[]{:S(2)}, u32[]{:S(2)}) collective-permute-start(bf16[128,1024]{1,0:T(8,128)(2,1)S(1)} %get-tuple-element.31), channel_id=1, source_target_pairs={{1,0},{2,1},{3,2},{5,4},{6,5},{7,6},{9,8},{10,9},{11,10},{13,12},{... | collective-permute-start | bytes 786440 | tf_op jit(solution)/shard_map/ppermute | solution.py:383
  38.6 1.3 %collective-permute-start.7 = (bf16[128,1024]{1,0:T(8,128)(2,1)S(1)}, bf16[128,1024]{1,0:T(8,128)(2,1)S(1)}, u32[]{:S(2)}, u32[]{:S(2)}) collective-permute-start(bf16[128,1024]{1,0:T(8,128)(2,1)S(1)} %get-tuple-element.32), channel_id=1, source_target_pairs={{2,0},{3,1},{6,4},{7,5},{10,8},{11,9},{14,12},{15,13},{18,16},{19,... | collective-permute-start | bytes 786440 | tf_op jit(solution)/shard_map/ppermute | solution.py:383
  39.9 1.3 %collective-permute-start.8 = (bf16[128,1024]{1,0:T(8,128)(2,1)S(1)}, bf16[128,1024]{1,0:T(8,128)(2,1)S(1)}, u32[]{:S(2)}, u32[]{:S(2)}) collective-permute-start(bf16[128,1024]{1,0:T(8,128)(2,1)S(1)} %get-tuple-element.33), channel_id=1, source_target_pairs={{3,0},{7,4},{11,8},{15,12},{19,16},{23,20},{27,24},{31,28}} | collective-permute-start | bytes 786440 | tf_op jit(solution)/shard_map/ppermute | solution.py:383
  41.2 15.2 %all_to_all.5.refs_4_ = f32[32,2,8]{2,1,0:T(2,128)S(1)} all-to-all(f32[32,2,8]{2,1,0:T(2,128)S(1)} %bitcast.22), channel_id=1, replica_groups=mesh['dp'=8,'ctx'=4] {'dp','ctx'}, dimensions={0} | all-to-all | bytes 4096 | tf_op jit(solution)/shard_map/all_to_all | solution.py:384
  56.5 0.9 %combine.1 = (bf16[128,512]{1,0:T(8,128)(2,1)}, bf16[128,512]{1,0:T(8,128)(2,1)}, f32[2,8]{1,0:T(2,128)}) custom-call(bf16[128,1024]{1,0:T(8,128)(2,1)S(1)} %get-tuple-element.30.refs_0_, bf16[128,1024]{1,0:T(8,128)(2,1)S(1)} %collective-permute-done.6.refs_1_, bf16[128,1024]{1,0:T(8,128)(2,1)S(1)} %collective-permute-done.7.refs_2_, ...), custom_call_target="tpu_custom_call" | custom-call | tf_op jit(solution)/shard_map/combine/pallas_call | solution.py:386
  (19 shorter events, 0.1 us)
Async XLA Ops:
  0.6 0.7 %copy-start.5 = (s32[1,128]{1,0:T(1,128)S(1)}, s32[1,128]{1,0:T(1,128)}, u32[]{:S(2)}) copy-start(s32[1,128]{1,0:T(1,128)} %depth_ref.5) | copy-start | bytes 1540
  0.6 0.7 %copy-start.6 = (s32[1,128]{1,0:T(1,128)S(1)}, s32[1,128]{1,0:T(1,128)}, u32[]{:S(2)}) copy-start(s32[1,128]{1,0:T(1,128)} %end_ref.5) | copy-start | bytes 1540
  1.3 0.9 %copy-start.3 = (bf16[1,128,512]{2,1,0:T(8,128)(2,1)S(1)}, bf16[1,128,512]{2,1,0:T(8,128)(2,1)}, u32[]{:S(2)}) copy-start(bf16[1,128,512]{2,1,0:T(8,128)(2,1)} %param.11) | copy-start | bytes 393220
  2.2 0.9 %copy-start.4 = (bf16[1,128,512]{2,1,0:T(8,128)(2,1)S(1)}, bf16[1,128,512]{2,1,0:T(8,128)(2,1)}, u32[]{:S(2)}) copy-start(bf16[1,128,512]{2,1,0:T(8,128)(2,1)} %param.12) | copy-start | bytes 393220
  3.2 12.2 %collective-permute-start.5 = (bf16[144,512]{1,0:T(8,128)(2,1)S(1)}, bf16[144,512]{1,0:T(8,128)(2,1)S(1)}, u32[]{:S(2)}, u32[]{:S(2)}) collective-permute-start(bf16[144,512]{1,0:T(8,128)(2,1)S(1)} %get-tuple-element.22), channel_id=1, source_target_pairs={{0,3},{4,7},{8,11},{12,15},{16,19},{20,23},{24,27},{28,31}} | collective-permute-start | bytes 442376 | tf_op jit(solution)/shard_map/ppermute | solution.py:308
  9.0 11.4 %collective-permute-start.4 = (bf16[144,512]{1,0:T(8,128)(2,1)S(1)}, bf16[144,512]{1,0:T(8,128)(2,1)S(1)}, u32[]{:S(2)}, u32[]{:S(2)}) collective-permute-start(bf16[144,512]{1,0:T(8,128)(2,1)S(1)} %get-tuple-element.22), channel_id=1, source_target_pairs={{0,2},{1,3},{4,6},{5,7},{8,10},{9,11},{12,14},{13,15},{16,18},{17,... | collective-permute-start | bytes 442376 | tf_op jit(solution)/shard_map/ppermute | solution.py:308
  10.3 10.1 %collective-permute-start.3 = (bf16[144,512]{1,0:T(8,128)(2,1)S(1)}, bf16[144,512]{1,0:T(8,128)(2,1)S(1)}, u32[]{:S(2)}, u32[]{:S(2)}) collective-permute-start(bf16[144,512]{1,0:T(8,128)(2,1)S(1)} %get-tuple-element.22), channel_id=1, source_target_pairs={{0,1},{1,2},{2,3},{4,5},{5,6},{6,7},{8,9},{9,10},{10,11},{12,13},{... | collective-permute-start | bytes 442376 | tf_op jit(solution)/shard_map/ppermute | solution.py:308
  12.8 18.2 %collective-permute-start.2 = (bf16[128,512]{1,0:T(8,128)(2,1)S(1)}, bf16[128,512]{1,0:T(8,128)(2,1)S(1)}, u32[]{:S(2)}, u32[]{:S(2)}) collective-permute-start(bf16[128,512]{1,0:T(8,128)(2,1)S(1)} %get-tuple-element.21), channel_id=1, source_target_pairs={{0,3},{4,7},{8,11},{12,15},{16,19},{20,23},{24,27},{28,31}} | collective-permute-start | bytes 393224 | tf_op jit(solution)/shard_map/ppermute | solution.py:308
  14.1 16.9 %collective-permute-start.1 = (bf16[128,512]{1,0:T(8,128)(2,1)S(1)}, bf16[128,512]{1,0:T(8,128)(2,1)S(1)}, u32[]{:S(2)}, u32[]{:S(2)}) collective-permute-start(bf16[128,512]{1,0:T(8,128)(2,1)S(1)} %get-tuple-element.21), channel_id=1, source_target_pairs={{0,2},{1,3},{4,6},{5,7},{8,10},{9,11},{12,14},{13,15},{16,18},{17,... | collective-permute-start | bytes 393224 | tf_op jit(solution)/shard_map/ppermute | solution.py:308
  15.4 15.6 %collective-permute-start = (bf16[128,512]{1,0:T(8,128)(2,1)S(1)}, bf16[128,512]{1,0:T(8,128)(2,1)S(1)}, u32[]{:S(2)}, u32[]{:S(2)}) collective-permute-start(bf16[128,512]{1,0:T(8,128)(2,1)S(1)} %get-tuple-element.21), channel_id=1, source_target_pairs={{0,1},{1,2},{2,3},{4,5},{5,6},{6,7},{8,9},{9,10},{10,11},{12,13},{... | collective-permute-start | bytes 393224 | tf_op jit(solution)/shard_map/ppermute | solution.py:308
  20.4 0.7 %copy-start.7 = (s32[1,8]{1,0:T(1,128)S(1)}, s32[1,8]{1,0:T(1,128)}, u32[]{:S(2)}) copy-start(s32[1,8]{1,0:T(1,128)} %lengths_ref.3) | copy-start | bytes 100
  20.4 0.7 %copy-start.8 = (f32[32]{0:T(128)S(1)}, f32[32]{0:T(128)}, u32[]{:S(2)}) copy-start(f32[32]{0:T(128)} %slope_ref.3) | copy-start | bytes 388
  20.4 0.7 %copy-start.9 = (f32[32]{0:T(128)S(1)}, f32[32]{0:T(128)}, u32[]{:S(2)}) copy-start(f32[32]{0:T(128)} %gain_ref.3) | copy-start | bytes 388
  21.1 1.2 %copy-start = (bf16[1,128,4096]{2,1,0:T(8,128)(2,1)S(1)}, bf16[1,128,4096]{2,1,0:T(8,128)(2,1)}, u32[]{:S(2)}) copy-start(bf16[1,128,4096]{2,1,0:T(8,128)(2,1)} %param.10) | copy-start | bytes 3145732
  22.3 1.2 %copy-start.1 = (bf16[1,128,4096]{2,1,0:T(8,128)(2,1)S(1)}, bf16[1,128,4096]{2,1,0:T(8,128)(2,1)}, u32[]{:S(2)}) copy-start(bf16[1,128,4096]{2,1,0:T(8,128)(2,1)} %param.13) | copy-start | bytes 3145732
  23.5 1.2 %copy-start.2 = (bf16[1,128,4096]{2,1,0:T(8,128)(2,1)S(1)}, bf16[1,128,4096]{2,1,0:T(8,128)(2,1)}, u32[]{:S(2)}) copy-start(bf16[1,128,4096]{2,1,0:T(8,128)(2,1)} %param.14) | copy-start | bytes 3145732
  37.3 19.1 %collective-permute-start.6 = (bf16[128,1024]{1,0:T(8,128)(2,1)S(1)}, bf16[128,1024]{1,0:T(8,128)(2,1)S(1)}, u32[]{:S(2)}, u32[]{:S(2)}) collective-permute-start(bf16[128,1024]{1,0:T(8,128)(2,1)S(1)} %get-tuple-element.31), channel_id=1, source_target_pairs={{1,0},{2,1},{3,2},{5,4},{6,5},{7,6},{9,8},{10,9},{11,10},{13,12},{... | collective-permute-start | bytes 786440 | tf_op jit(solution)/shard_map/ppermute | solution.py:383
  38.6 17.8 %collective-permute-start.7 = (bf16[128,1024]{1,0:T(8,128)(2,1)S(1)}, bf16[128,1024]{1,0:T(8,128)(2,1)S(1)}, u32[]{:S(2)}, u32[]{:S(2)}) collective-permute-start(bf16[128,1024]{1,0:T(8,128)(2,1)S(1)} %get-tuple-element.32), channel_id=1, source_target_pairs={{2,0},{3,1},{6,4},{7,5},{10,8},{11,9},{14,12},{15,13},{18,16},{19,... | collective-permute-start | bytes 786440 | tf_op jit(solution)/shard_map/ppermute | solution.py:383
  39.9 16.6 %collective-permute-start.8 = (bf16[128,1024]{1,0:T(8,128)(2,1)S(1)}, bf16[128,1024]{1,0:T(8,128)(2,1)S(1)}, u32[]{:S(2)}, u32[]{:S(2)}) collective-permute-start(bf16[128,1024]{1,0:T(8,128)(2,1)S(1)} %get-tuple-element.33), channel_id=1, source_target_pairs={{3,0},{7,4},{11,8},{15,12},{19,16},{23,20},{27,24},{31,28}} | collective-permute-start | bytes 786440 | tf_op jit(solution)/shard_map/ppermute | solution.py:383
where the time goes:
time: 57.8 us; the launch traced here: 57.3 us
  starting transfers between devices  17.3 us (30%)
  blocking collectives  15.2 us (26%)
  Pallas kernels  13.5 us (23%)
  local copies, waits for them, and re-layouts  6.82 us (12%)
  waiting for transfers between devices  3.73 us (6%)
  between operations  0.75 us (1%)
    all_to_all x1, blocking collectives, body(): lax.all_to_all(bias_parts, ('dp', 'ctx'), split_axis=0, concat_axis=0, ti...  15.2 us
    ppermute x6, starting transfers between devices, body(): lax.ppermute(message, 'ctx', [(i, i + shift) for i in range(blocks - shif...  13.5 us
    pallas_call x2, Pallas kernels, body(): pl.pallas_call(functools.partial(main_kernel, blocks, heads_per_group, bl...  12.5 us
    unnamed x20, local copies, waits for them, and re-layouts  6.82 us
    ppermute x3, starting transfers between devices, body(): parts[shift] = lax.ppermute(parts[shift], 'ctx', back)  3.86 us
    ppermute x6, waiting for transfers between devices, body(): lax.ppermute(message, 'ctx', [(i, i + shift) for i in range(blocks - shif...  3.72 us
  transfers between devices with their start and end apart: 9, of which 1 were waited for; matrix products, arithmetic and copies ran while one was open for 0% of the time, Pallas kernels for 11%

commit v1 on v0

v1 whole, which is shorter than its diff:
```python
import functools

import jax
import jax.numpy as jnp
from jax import lax
from jax.experimental import pallas as pl
from jax.experimental.pallas import tpu as pltpu
from jax.sharding import PartitionSpec as P

WIDTH = 128
LOG2E = 1.4426950408889634
MASKED = -1e30
META_ROWS = 16
END_UNIT = 64
CHUNKS = 2
QUAD = 4

VMEM_LIMIT = 32 * 1024 * 1024


def dot_nt(a, b):
    return lax.dot_general(a, b, (((1,), (1,)), ((), ())), preferred_element_type=jnp.float32)


def dot_nn(a, b):
    return lax.dot_general(a, b, (((1,), (0,)), ((), ())), preferred_element_type=jnp.float32)


def pack_kernel(key_ref, value_ref, depth_ref, end_ref, *message_refs):
    tokens = key_ref.shape[0]
    groups = key_ref.shape[1] // WIDTH // len(message_refs)
    for chunk, message_ref in enumerate(message_refs):
        for group in range(groups):
            source = slice((chunk * groups + group) * WIDTH, (chunk * groups + group + 1) * WIDTH)
            at = 2 * group * WIDTH
            message_ref[0:tokens, at : at + WIDTH] = key_ref[:, source]
            message_ref[0:tokens, at + WIDTH : at + 2 * WIDTH] = value_ref[:, source]
    depth = depth_ref[...]
    end = end_ref[...]
    end_high = end // END_UNIT
    end_low = end - end_high * END_UNIT
    row = lax.broadcasted_iota(jnp.int32, (META_ROWS, tokens), 0)
    meta = jnp.where(row == 0, depth, jnp.where(row == 1, end_high, end_low))
    meta = meta.astype(jnp.float32).astype(jnp.bfloat16)
    below = slice(tokens, tokens + META_ROWS)
    message_refs[0][below, 0:tokens] = meta
    message_refs[0][below, tokens:] = jnp.zeros(
        (META_ROWS, 2 * groups * WIDTH - tokens), jnp.bfloat16
    )


def as_column(row):
    size = row.shape[1]
    return jnp.transpose(jnp.broadcast_to(row, (size, size)))


def dot_tn(a, b):
    return lax.dot_general(a, b, (((0,), (0,)), ((), ())), preferred_element_type=jnp.float32)


def fold_rows(block):
    return jnp.sum(block.reshape(block.shape[0] // 8, 8, block.shape[1]), axis=0)


def main_kernel(
    blocks,
    heads_per_group,
    groups,
    first_group,
    unroll,
    lengths_ref,
    slope_ref,
    gain_ref,
    depth_ref,
    end_ref,
    query_hbm,
    output_hbm,
    grad_hbm,
    key_hbm,
    value_hbm,
    *refs,
):
    tokens = query_hbm.shape[0]
    remote = refs[0 : blocks - 1]
    remote_meta = refs[blocks - 1 : 2 * (blocks - 1)]
    rest = refs[2 * (blocks - 1) :]
    if first_group:
        bias_before = rest[0]
        parts_before = rest[1 : 1 + blocks]
        rest = rest[2 + blocks :]
    query_grad_hbm = rest[0]
    part_refs = rest[1 : 1 + blocks]
    bias_ref = rest[1 + blocks]
    (
        query_ref,
        output_ref,
        grad_ref,
        key_ref,
        value_ref,
        query_grad_ref,
        distance_ref,
        ancestor_ref,
        slope_rows,
        gain_rows,
        key_acc,
        value_acc,
        weight_ref,
        probs_ref,
        dscore_ref,
        load_sems,
        store_sems,
    ) = rest[2 + blocks :]
    factor = WIDTH**-0.5
    group_columns = heads_per_group * WIDTH
    quads = heads_per_group // QUAD

    loads = []
    for group in range(groups):
        at = first_group + group
        wide = pl.ds(at * group_columns, group_columns)
        thin = pl.ds(at * WIDTH, WIDTH)
        pairs = [
            (query_hbm.at[:, wide], query_ref.at[group]),
            (key_hbm.at[:, thin], key_ref.at[group]),
            (output_hbm.at[:, wide], output_ref.at[group]),
            (grad_hbm.at[:, wide], grad_ref.at[group]),
            (value_hbm.at[:, thin], value_ref.at[group]),
        ]
        loads.append(
            [
                pltpu.make_async_copy(source, to, load_sems.at[group, i])
                for i, (source, to) in enumerate(pairs)
            ]
        )
        for load in loads[-1]:
            load.start()

    here = lax.axis_index("ctx")
    query_pos = here * tokens + lax.broadcasted_iota(jnp.int32, (tokens, tokens), 1)
    start = jnp.zeros((tokens, tokens), jnp.int32)
    bound = jnp.int32(0)
    for index in range(lengths_ref.shape[1]):
        bound = bound + lengths_ref[0, index]
        start = jnp.where(query_pos >= bound, bound, start)
    query_depth = jnp.broadcast_to(depth_ref[...].astype(jnp.float32), (tokens, tokens))
    for shift in range(blocks):
        key_pos = (here ^ shift) * tokens + lax.broadcasted_iota(jnp.int32, (tokens, tokens), 0)
        if shift == 0:
            key_depth = as_column(depth_ref[...].astype(jnp.float32))
            key_end = as_column(end_ref[...].astype(jnp.float32))
        else:
            meta = remote_meta[shift - 1][tokens : tokens + META_ROWS, 0:tokens]
            meta = meta.astype(jnp.float32)
            key_depth = as_column(meta[0:1])
            key_end = as_column(meta[1:2] * END_UNIT + meta[2:3])
        inside = query_pos.astype(jnp.float32) < key_end
        allowed = (key_pos <= query_pos) & (key_pos >= start)
        rows = slice(shift * tokens, (shift + 1) * tokens)
        distance_ref[rows, :] = jnp.abs(query_depth - key_depth)
        ancestor_ref[rows, :] = jnp.where(allowed, jnp.where(inside, 1.0, 0.0), MASKED)

    block_rows = [slice(shift * tokens, (shift + 1) * tokens) for shift in range(blocks)]

    def stacked(ref, group, first, count):
        heads = [first + i for i in range(count)]
        return jnp.concatenate([ref[group, :, h * WIDTH : (h + 1) * WIDTH] for h in heads], axis=0)

    def scores(group, keys, value_ext, first, slot, place):
        query_pair = stacked(query_ref, group, first, 2)
        grad_pair = stacked(grad_ref, group, first, 2)
        output_pair = stacked(output_ref, group, first, 2)
        grad_ext = jnp.concatenate([grad_pair, grad_pair * output_pair], axis=1)
        raw = dot_nt(keys, query_pair)
        scales = []
        for half in range(2):
            head = (first_group + group) * heads_per_group + first + half
            gain = gain_ref[head] * LOG2E
            slope = slope_ref[head] * LOG2E
            lanes = slice(half * tokens, (half + 1) * tokens)
            tops, totals = [], []
            for rows in block_rows:
                score = raw[rows, lanes] * (factor * LOG2E) + (
                    gain * ancestor_ref[rows, :] - slope * distance_ref[rows, :]
                )
                top = jnp.max(score, axis=0, keepdims=True)
                weight = jnp.exp2(score - top)
                weight_ref[slot, rows, lanes] = weight
                tops.append(top)
                totals.append(jnp.sum(weight, axis=0, keepdims=True))
            top = functools.reduce(jnp.maximum, tops)
            shrink = [jnp.exp2(t - top) for t in tops]
            total = sum(a * b for a, b in zip(totals, shrink))
            inverse = 1.0 / total
            scales.append([s * inverse for s in shrink])
        centred = dot_nt(value_ext, grad_ext)
        for half in range(2):
            lanes = slice(half * tokens, (half + 1) * tokens)
            to = slice((place + half) * tokens, (place + half + 1) * tokens)
            slope_sum, gain_sum = 0.0, 0.0
            for rows, scale in zip(block_rows, scales[half]):
                probs = weight_ref[slot, rows, lanes] * scale
                dscore = probs * centred[rows, lanes]
                probs_ref[slot, rows, to] = probs.astype(jnp.bfloat16)
                dscore_ref[slot, rows, to] = dscore.astype(jnp.bfloat16)
                slope_sum = slope_sum + fold_rows(dscore * distance_ref[rows, :])
                gain_sum = gain_sum + fold_rows(dscore * ancestor_ref[rows, :])
            at = group * heads_per_group + first + half
            slope_rows[at : at + 1, :] = -jnp.sum(slope_sum, axis=0, keepdims=True)
            gain_rows[at : at + 1, :] = jnp.sum(gain_sum, axis=0, keepdims=True)

    def gradients(group, keys, quad, slot):
        query_quad = stacked(query_ref, group, quad * QUAD, QUAD)
        grad_quad = stacked(grad_ref, group, quad * QUAD, QUAD)
        dscore_b = dscore_ref[slot]
        key_part = dot_nn(dscore_b, query_quad)
        value_part = dot_nn(probs_ref[slot], grad_quad)
        if quad == 0:
            key_acc[group] = key_part
            value_acc[group] = value_part
        else:
            key_acc[group] += key_part
            value_acc[group] += value_part
        query_part = (dot_tn(dscore_b, keys) * factor).astype(jnp.bfloat16)
        for i in range(QUAD):
            at = (quad * QUAD + i) * WIDTH
            query_grad_ref[group, :, at : at + WIDTH] = query_part[i * tokens : (i + 1) * tokens]
        if quad == quads - 1:
            for shift, rows in enumerate(block_rows):
                at = 2 * group * WIDTH
                if first_group:
                    at = at + parts_before[shift].shape[1]
                key_block = (key_acc[group, rows, :] * factor).astype(jnp.bfloat16)
                part_refs[shift][:, at : at + WIDTH] = key_block
                value_block = value_acc[group, rows, :].astype(jnp.bfloat16)
                part_refs[shift][:, at + WIDTH : at + 2 * WIDTH] = value_block

    stores = []
    for group in range(groups):
        wide = pl.ds((first_group + group) * group_columns, group_columns)
        stores.append(
            pltpu.make_async_copy(
                query_grad_ref.at[group], query_grad_hbm.at[:, wide], store_sems.at[group]
            )
        )
    waiting = None
    step = 0
    for group in range(groups):
        for load in loads[group]:
            load.wait()
        at = slice(2 * group * WIDTH, (2 * group + 1) * WIDTH)
        keys = jnp.concatenate([key_ref[group]] + [r[0:tokens, at] for r in remote], axis=0)
        at = slice((2 * group + 1) * WIDTH, (2 * group + 2) * WIDTH)
        values = jnp.concatenate([value_ref[group]] + [r[0:tokens, at] for r in remote], axis=0)
        value_ext = jnp.concatenate([values, jnp.full(values.shape, -1.0, jnp.bfloat16)], axis=1)
        for quad in range(quads):
            slot = step % 2
            for place in range(0, QUAD, 2):
                scores(group, keys, value_ext, quad * QUAD + place, slot, place)
            if waiting is not None:
                gradients(*waiting)
                if waiting[2] == quads - 1:
                    stores[waiting[0]].start()
            waiting = (group, keys, quad, slot)
            step += 1
    gradients(*waiting)
    stores[waiting[0]].start()

    if first_group:
        for shift in range(blocks):
            before = parts_before[shift]
            part_refs[shift][:, 0 : before.shape[1]] = before[...]
    slope_sum = jnp.sum(slope_rows[...], axis=1, keepdims=True)
    gain_sum = jnp.sum(gain_rows[...], axis=1, keepdims=True)
    shape = slope_rows.shape
    lane = lax.broadcasted_iota(jnp.int32, shape, 1)
    row = lax.broadcasted_iota(jnp.int32, shape, 0)
    replicas, parts, rows_here, local = bias_ref.shape
    local_heads = slope_ref.shape[0] // parts
    kind = lax.broadcasted_iota(jnp.int32, (rows_here, local), 0)
    for part in range(parts):
        mine = lane == row - part * local_heads + first_group * heads_per_group
        mine = mine & (lane < local_heads)
        slope_line = jnp.sum(jnp.where(mine, slope_sum, 0.0), axis=0, keepdims=True)
        gain_line = jnp.sum(jnp.where(mine, gain_sum, 0.0), axis=0, keepdims=True)
        tile = jnp.where(kind == 0, slope_line, jnp.where(kind == 1, gain_line, 0.0))
        if first_group:
            tile = tile + bias_before[0, part]
        bias_ref[:, part] = jnp.broadcast_to(tile[None], (replicas, rows_here, local))
    for store in stores:
        store.wait()


def final_kernel(blocks, *refs):
    parts = refs[0:blocks]
    bias_parts, key_out, value_out, bias_out = refs[blocks:]
    for group in range(key_out.shape[1] // WIDTH):
        to = slice(group * WIDTH, (group + 1) * WIDTH)
        for kind, out in enumerate((key_out, value_out)):
            at = (2 * group + kind) * WIDTH
            total = parts[0][:, at : at + WIDTH].astype(jnp.float32)
            for shift in range(1, blocks):
                total = total + parts[shift][:, at : at + WIDTH].astype(jnp.float32)
            out[:, to] = total.astype(jnp.bfloat16)
    bias_out[...] = jnp.sum(bias_parts[...], axis=0)[0:2, 0 : bias_out.shape[1]]


def gather_blocks(messages, blocks):
    if blocks != 4:
        return [
            [
                lax.ppermute(m, "ctx", [(i, i ^ s) for i in range(blocks) if i < i ^ s])
                for s in range(1, blocks)
            ]
            for m in messages
        ]
    turns = [turn % 2 for turn in range(len(messages))]
    x_pairs = [[(0, 1), (2, 3)], [(0, 1), (1, 0), (2, 3)]]
    along_x = [lax.ppermute(m, "ctx", x_pairs[t]) for m, t in zip(messages, turns)]
    along_y = [lax.ppermute(m, "ctx", [(0, 2), (1, 3)]) for m in messages]
    passed_on = [
        lax.ppermute(x, "ctx", [(0, 2), (1, 3)]) if t else lax.ppermute(y, "ctx", [(2, 3), (3, 2)])
        for x, y, t in zip(along_x, along_y, turns)
    ]
    return [list(three) for three in zip(along_x, along_y, passed_on)]


def body(
    queries,
    key_rows,
    values,
    outputs,
    out_grads,
    depths,
    subtree_end,
    file_lengths,
    slopes,
    ancestor_gain,
):
    blocks = lax.axis_size("ctx")
    replicas = lax.axis_size("dp")
    tokens, width_all = queries.shape[1:]
    kv_width = key_rows.shape[2]
    heads_all = width_all // WIDTH
    kv_heads = kv_width // WIDTH
    heads_per_group = heads_all // kv_heads
    group_columns = heads_per_group * WIDTH
    local_heads = heads_all // blocks
    keys_seen = blocks * tokens
    groups = kv_heads // CHUNKS
    bf16, f32 = jnp.bfloat16, jnp.float32
    vmem = pl.BlockSpec(memory_space=pltpu.VMEM)
    smem = pl.BlockSpec(memory_space=pltpu.SMEM)
    anywhere = pl.BlockSpec(memory_space=pl.ANY)
    params = pltpu.CompilerParams(vmem_limit_bytes=VMEM_LIMIT)

    def hold(array):
        return pltpu.with_memory_space_constraint(array, pltpu.HBM)

    key_held, value_held = hold(key_rows[0]), hold(values[0])
    depth_held, end_held = hold(depths), hold(subtree_end)
    messages = pl.pallas_call(
        pack_kernel,
        out_shape=[
            jax.ShapeDtypeStruct(
                (tokens + (META_ROWS if chunk == 0 else 0), 2 * groups * WIDTH), bf16
            )
            for chunk in range(CHUNKS)
        ],
        in_specs=[vmem] * 4,
        out_specs=[vmem] * CHUNKS,
        compiler_params=params,
        name="pack",
    )(key_held, value_held, depth_held, end_held)
    arrived = gather_blocks(messages, blocks)

    bias_shape = (replicas, blocks, 8, WIDTH)
    matmul_flops = 2 * tokens * keys_seen * WIDTH * heads_all
    results = None
    for chunk in range(CHUNKS):
        operands = [
            hold(file_lengths),
            hold(slopes),
            hold(ancestor_gain),
            depth_held,
            end_held,
            hold(queries[0]),
            hold(outputs[0]),
            hold(out_grads[0]),
            key_held,
            value_held,
            *arrived[chunk],
            *arrived[0],
        ]
        specs = [smem] * 3 + [vmem] * 2 + [anywhere] * 5 + [vmem] * (2 * blocks - 2)
        aliases = {}
        if chunk:
            operands = operands + [results[1 + blocks], *results[1 : 1 + blocks], results[0]]
            specs = specs + [vmem] * (1 + blocks) + [anywhere]
            aliases = {len(operands) - 1: 0}
        part_shape = (tokens, 2 * (chunk + 1) * groups * WIDTH)
        results = pl.pallas_call(
            functools.partial(
                main_kernel, blocks, heads_per_group, groups, chunk * groups, blocks <= 4
            ),
            out_shape=[jax.ShapeDtypeStruct((tokens, width_all), bf16)]
            + [jax.ShapeDtypeStruct(part_shape, bf16)] * blocks
            + [jax.ShapeDtypeStruct(bias_shape, f32)],
            in_specs=specs,
            out_specs=[anywhere] + [vmem] * (1 + blocks),
            scratch_shapes=[
                pltpu.VMEM((groups, tokens, group_columns), bf16),
                pltpu.VMEM((groups, tokens, group_columns), bf16),
                pltpu.VMEM((groups, tokens, group_columns), bf16),
                pltpu.VMEM((groups, tokens, WIDTH), bf16),
                pltpu.VMEM((groups, tokens, WIDTH), bf16),
                pltpu.VMEM((groups, tokens, group_columns), bf16),
                pltpu.VMEM((keys_seen, tokens), f32),
                pltpu.VMEM((keys_seen, tokens), f32),
                pltpu.VMEM((groups * heads_per_group, tokens), f32),
                pltpu.VMEM((groups * heads_per_group, tokens), f32),
                pltpu.VMEM((groups, keys_seen, WIDTH), f32),
                pltpu.VMEM((groups, keys_seen, WIDTH), f32),
                pltpu.VMEM((2, keys_seen, 2 * tokens), f32),
                pltpu.VMEM((2, keys_seen, QUAD * tokens), bf16),
                pltpu.VMEM((2, keys_seen, QUAD * tokens), bf16),
                pltpu.SemaphoreType.DMA((groups, 5)),
                pltpu.SemaphoreType.DMA((groups,)),
            ],
            input_output_aliases=aliases,
            compiler_params=params,
            cost_estimate=pl.CostEstimate(
                flops=5 * matmul_flops // CHUNKS,
                bytes_accessed=10 * tokens * width_all // CHUNKS,
                transcendentals=tokens * keys_seen * heads_all // CHUNKS,
            ),
            name=f"attend_{chunk}",
        )(*operands)
    query_grads = results[0]
    parts = list(results[1 : 1 + blocks])
    bias_parts = results[1 + blocks].reshape(replicas * blocks, 8, WIDTH)
    for shift in range(1, blocks):
        back = [(i, i ^ shift) for i in range(blocks) if i > i ^ shift]
        parts[shift] = lax.ppermute(parts[shift], "ctx", back)
    bias_parts = lax.all_to_all(bias_parts, ("dp", "ctx"), split_axis=0, concat_axis=0, tiled=True)

    key_grads, value_grads, bias_grads = pl.pallas_call(
        functools.partial(final_kernel, blocks),
        out_shape=[
            jax.ShapeDtypeStruct((tokens, kv_width), bf16),
            jax.ShapeDtypeStruct((tokens, kv_width), bf16),
            jax.ShapeDtypeStruct((2, local_heads), f32),
        ],
        in_specs=[vmem] * (blocks + 1),
        out_specs=[vmem] * 3,
        compiler_params=params,
        name="combine",
    )(*parts, bias_parts)
    return (query_grads[None], key_grads[None], value_grads[None], bias_grads.T)


def solution(mesh):
    in_specs = (
        P("dp", "ctx", None),
        P("dp", "ctx", None),
        P("dp", "ctx", None),
        P("dp", "ctx", None),
        P("dp", "ctx", None),
        P("dp", "ctx"),
        P("dp", "ctx"),
        P("dp", None),
        P(),
        P(),
    )
    out_specs = (P("dp", "ctx", None), P("dp", "ctx", None), P("dp", "ctx", None), P("ctx", None))
    return jax.shard_map(body, mesh=mesh, in_specs=in_specs, out_specs=out_specs, check_vma=False)
```

time: 57.8 us -> 59.1 us (1.022)
  starting transfers between devices: 17.3 us -> 25 us
  local copies, waits for them, and re-layouts: 6.82 us -> 0 us
  waiting for transfers between devices: 3.73 us -> 0.02 us
  Pallas kernels: 13.5 us -> 16.6 us
  blocking collectives: 15.2 us -> 16.4 us
    ppermute x6, starting transfers between devices: 13.5 us -> 21.1 us  [the longest x2 11 us: gather_blocks(): along_y = [lax.ppermute(m, 'ctx', [(0, 2), (1, 3)]) for m in messages]]
    unnamed x20 -> x0, local copies, waits for them, and re-layouts: 6.82 us -> none
    ppermute x6, waiting for transfers between devices: 3.72 us -> 0.02 us  [the longest x2 0.01 us: gather_blocks(): along_y = [lax.ppermute(m, 'ctx', [(0, 2), (1, 3)]) for m in messages]]
    pallas_call x2, Pallas kernels: 12.5 us -> 14.7 us  [body(): pl.pallas_call(functools.partial(main_kernel, blocks, heads_per_group, gr...]
    all_to_all x1, blocking collectives: 15.2 us -> 16.4 us  [body(): lax.all_to_all(bias_parts, ('dp', 'ctx'), split_axis=0, concat_axis=0, ti...]
    pallas_call x1, Pallas kernels: 0.06 us -> 1.03 us  [body(): pl.pallas_call(pack_kernel, out_shape=[jax.ShapeDtypeStruct((tokens + (ME...]
  transfers between devices with their start and end apart: 9 -> 9, of which waited for: 1 -> 0; matrix products, arithmetic and copies ran while one was open for 0% -> 0% of each run, Pallas kernels for 11% -> 12%
where the time goes in v1:
time: 59.1 us; the launch traced here: 58.8 us
  starting transfers between devices  25 us (42%)
  Pallas kernels  16.6 us (28%)
  blocking collectives  16.4 us (28%)
  between operations  0.77 us (1%)
    all_to_all x1, blocking collectives, body(): lax.all_to_all(bias_parts, ('dp', 'ctx'), split_axis=0, concat_axis=0, ti...  16.4 us
    pallas_call x2, Pallas kernels, body(): pl.pallas_call(functools.partial(main_kernel, blocks, heads_per_group, gr...  14.7 us
    ppermute x2, starting transfers between devices, gather_blocks(): along_y = [lax.ppermute(m, 'ctx', [(0, 2), (1, 3)]) for m in messages]  11 us
    ppermute x2, starting transfers between devices, gather_blocks(): lax.ppermute(m, 'ctx', x_pairs[t])  6.45 us
    ppermute x3, starting transfers between devices, body(): parts[shift] = lax.ppermute(parts[shift], 'ctx', back)  3.88 us
    ppermute x1, starting transfers between devices, gather_blocks(): lax.ppermute(x, 'ctx', [(0, 2), (1, 3)])  2.96 us
  transfers between devices with their start and end apart: 9, of which 0 were waited for; matrix products, arithmetic and copies ran while one was open for 0% of the time, Pallas kernels for 12%

profile of v1, /device:TPU:0, one launch (start us, length us, event | category | flops | bytes accessed | tf_op | source)
XLA Modules:
  0.0 58.8 jit_solution(18266572025889145449)
XLA Ops:
  0.6 1.0 %pack.1 = (bf16[144,512]{1,0:T(8,128)(2,1)S(1)}, bf16[128,512]{1,0:T(8,128)(2,1)S(1)}) custom-call(bf16[128,512]{1,0:T(8,128)(2,1)} %bitcast.18, bf16[128,512]{1,0:T(8,128)(2,1)} %bitcast.21, s32[1,128]{1,0:T(1,128)} %depth_ref.5, s32[1,128]{1,0:T(1,128)} %end_ref.5), custom_call_target="tpu_custom_call" | custom-call | tf_op jit(solution)/shard_map/pack/pallas_call | solution.py:361
  1.7 4.9 %collective-permute-start.4 = (bf16[144,512]{1,0:T(8,128)(2,1)S(1)}, bf16[144,512]{1,0:T(8,128)(2,1)S(1)}, u32[]{:S(2)}, u32[]{:S(2)}) collective-permute-start(bf16[144,512]{1,0:T(8,128)(2,1)S(1)} %get-tuple-element.22), channel_id=1, source_target_pairs={{0,2},{1,3},{4,6},{5,7},{8,10},{9,11},{12,14},{13,15},{16,18},{17,... | collective-permute-start | bytes 442376 | tf_op jit(solution)/shard_map/ppermute | solution.py:319
  6.6 3.4 %collective-permute-start.3 = (bf16[144,512]{1,0:T(8,128)(2,1)S(1)}, bf16[144,512]{1,0:T(8,128)(2,1)S(1)}, u32[]{:S(2)}, u32[]{:S(2)}) collective-permute-start(bf16[144,512]{1,0:T(8,128)(2,1)S(1)} %get-tuple-element.22), channel_id=1, source_target_pairs={{0,1},{2,3},{4,5},{6,7},{8,9},{10,11},{12,13},{14,15},{16,17},{18,... | collective-permute-start | bytes 442376 | tf_op jit(solution)/shard_map/ppermute | solution.py:318
  10.0 0.0 collective-permute-done.4.refs_1_.refs_4_
  10.0 0.7 %collective-permute-start.5 = (bf16[144,512]{1,0:T(8,128)(2,1)S(1)}, bf16[144,512]{1,0:T(8,128)(2,1)S(1)}, u32[]{:S(2)}, u32[]{:S(2)}) collective-permute-start(bf16[144,512]{1,0:T(8,128)(2,1)S(1)} %collective-permute-done.4.refs_1_.refs_4_), channel_id=1, source_target_pairs={{2,3},{3,2},{6,7},{7,6},{10,11},{11,10},{14,15},{15,14},{18,19},{1... | collective-permute-start | bytes 442376 | tf_op jit(solution)/shard_map/ppermute | solution.py:321
  10.7 3.0 %collective-permute-start = (bf16[128,512]{1,0:T(8,128)(2,1)S(1)}, bf16[128,512]{1,0:T(8,128)(2,1)S(1)}, u32[]{:S(2)}, u32[]{:S(2)}) collective-permute-start(bf16[128,512]{1,0:T(8,128)(2,1)S(1)} %get-tuple-element.21), channel_id=1, source_target_pairs={{0,1},{1,0},{2,3},{4,5},{5,4},{6,7},{8,9},{9,8},{10,11},{12,13},{1... | collective-permute-start | bytes 393224 | tf_op jit(solution)/shard_map/ppermute | solution.py:318
  13.7 6.2 %collective-permute-start.1 = (bf16[128,512]{1,0:T(8,128)(2,1)S(1)}, bf16[128,512]{1,0:T(8,128)(2,1)S(1)}, u32[]{:S(2)}, u32[]{:S(2)}) collective-permute-start(bf16[128,512]{1,0:T(8,128)(2,1)S(1)} %get-tuple-element.21), channel_id=1, source_target_pairs={{0,2},{1,3},{4,6},{5,7},{8,10},{9,11},{12,14},{13,15},{16,18},{17,... | collective-permute-start | bytes 393224 | tf_op jit(solution)/shard_map/ppermute | solution.py:319
  19.9 0.0 collective-permute-done.refs_0_
  19.9 3.0 %collective-permute-start.2 = (bf16[128,512]{1,0:T(8,128)(2,1)S(1)}, bf16[128,512]{1,0:T(8,128)(2,1)S(1)}, u32[]{:S(2)}, u32[]{:S(2)}) collective-permute-start(bf16[128,512]{1,0:T(8,128)(2,1)S(1)} %collective-permute-done.refs_0_), channel_id=1, source_target_pairs={{0,2},{1,3},{4,6},{5,7},{8,10},{9,11},{12,14},{13,15},{16,18},{17,... | collective-permute-start | bytes 393224 | tf_op jit(solution)/shard_map/ppermute | solution.py:321
  22.9 0.0 collective-permute-done.3.refs_0_.refs_3_
  22.9 0.0 collective-permute-done.5.refs_2_.refs_5_
  22.9 7.3 %attend_0.1 = (bf16[128,4096]{1,0:T(8,128)(2,1)}, bf16[128,512]{1,0:T(8,128)(2,1)S(1)}, bf16[128,512]{1,0:T(8,128)(2,1)S(1)}, bf16[128,512]{1,0:T(8,128)(2,1)S(1...) custom-call(s32[1,8]{1,0:T(1,128)} %lengths_ref.3, f32[32]{0:T(128)} %slope_ref.3, f32[32]{0:T(128)} %gain_ref.3, ...), custom_call_target="tpu_custom_call" | custom-call | flops 1342177280 | bytes 2621440 | tf_op jit(solution)/shard_map/attend_0/pallas_call | solution.py:401
  30.2 0.0 collective-permute-done.1.refs_1_
  30.2 0.0 collective-permute-done.2.refs_2_
  30.2 7.4 %attend_1.1 = (bf16[128,4096]{1,0:T(8,128)(2,1)}, bf16[128,1024]{1,0:T(8,128)(2,1)S(1)}, bf16[128,1024]{1,0:T(8,128)(2,1)S(1)}, bf16[128,1024]{1,0:T(8,128)(2,1)...) custom-call(s32[1,8]{1,0:T(1,128)} %lengths_ref.3, ...), custom_call_target="tpu_custom_call", output_to_operand_aliasing={{0}: (21, {})} | custom-call | flops 1342177280 | bytes 2621440 | tf_op jit(solution)/shard_map/attend_1/pallas_call | solution.py:401
  37.6 1.3 %collective-permute-start.6 = (bf16[128,1024]{1,0:T(8,128)(2,1)S(1)}, bf16[128,1024]{1,0:T(8,128)(2,1)S(1)}, u32[]{:S(2)}, u32[]{:S(2)}) collective-permute-start(bf16[128,1024]{1,0:T(8,128)(2,1)S(1)} %get-tuple-element.31), channel_id=1, source_target_pairs={{1,0},{3,2},{5,4},{7,6},{9,8},{11,10},{13,12},{15,14},{17,16},{19,... | collective-permute-start | bytes 786440 | tf_op jit(solution)/shard_map/ppermute | solution.py:443
  38.9 1.3 %collective-permute-start.7 = (bf16[128,1024]{1,0:T(8,128)(2,1)S(1)}, bf16[128,1024]{1,0:T(8,128)(2,1)S(1)}, u32[]{:S(2)}, u32[]{:S(2)}) collective-permute-start(bf16[128,1024]{1,0:T(8,128)(2,1)S(1)} %get-tuple-element.32), channel_id=1, source_target_pairs={{2,0},{3,1},{6,4},{7,5},{10,8},{11,9},{14,12},{15,13},{18,16},{19,... | collective-permute-start | bytes 786440 | tf_op jit(solution)/shard_map/ppermute | solution.py:443
  40.2 1.3 %collective-permute-start.8 = (bf16[128,1024]{1,0:T(8,128)(2,1)S(1)}, bf16[128,1024]{1,0:T(8,128)(2,1)S(1)}, u32[]{:S(2)}, u32[]{:S(2)}) collective-permute-start(bf16[128,1024]{1,0:T(8,128)(2,1)S(1)} %get-tuple-element.33), channel_id=1, source_target_pairs={{2,1},{3,0},{6,5},{7,4},{10,9},{11,8},{14,13},{15,12},{18,17},{19,... | collective-permute-start | bytes 786440 | tf_op jit(solution)/shard_map/ppermute | solution.py:443
  41.5 16.4 %all_to_all.5.refs_4_ = f32[32,8,128]{2,1,0:T(8,128)S(1)} all-to-all(f32[32,8,128]{2,1,0:T(8,128)S(1)} %bitcast.10), channel_id=1, replica_groups=mesh['dp'=8,'ctx'=4] {'dp','ctx'}, dimensions={0} | all-to-all | bytes 262144 | tf_op jit(solution)/shard_map/all_to_all | solution.py:444
  57.9 0.0 collective-permute-done.6.refs_1_
  57.9 0.0 collective-permute-done.7.refs_2_
  57.9 0.0 collective-permute-done.8.refs_3_
  57.9 0.9 %combine.1 = (bf16[128,512]{1,0:T(8,128)(2,1)}, bf16[128,512]{1,0:T(8,128)(2,1)}, f32[2,8]{1,0:T(2,128)}) custom-call(bf16[128,1024]{1,0:T(8,128)(2,1)S(1)} %get-tuple-element.30.refs_0_, bf16[128,1024]{1,0:T(8,128)(2,1)S(1)} %collective-permute-done.6.refs_1_, bf16[128,1024]{1,0:T(8,128)(2,1)S(1)} %collective-permute-done.7.refs_2_, ...), custom_call_target="tpu_custom_call" | custom-call | tf_op jit(solution)/shard_map/combine/pallas_call | solution.py:446
Async XLA Ops:
  1.7 8.3 %collective-permute-start.4 = (bf16[144,512]{1,0:T(8,128)(2,1)S(1)}, bf16[144,512]{1,0:T(8,128)(2,1)S(1)}, u32[]{:S(2)}, u32[]{:S(2)}) collective-permute-start(bf16[144,512]{1,0:T(8,128)(2,1)S(1)} %get-tuple-element.22), channel_id=1, source_target_pairs={{0,2},{1,3},{4,6},{5,7},{8,10},{9,11},{12,14},{13,15},{16,18},{17,... | collective-permute-start | bytes 442376 | tf_op jit(solution)/shard_map/ppermute | solution.py:319
  6.6 16.3 %collective-permute-start.3 = (bf16[144,512]{1,0:T(8,128)(2,1)S(1)}, bf16[144,512]{1,0:T(8,128)(2,1)S(1)}, u32[]{:S(2)}, u32[]{:S(2)}) collective-permute-start(bf16[144,512]{1,0:T(8,128)(2,1)S(1)} %get-tuple-element.22), channel_id=1, source_target_pairs={{0,1},{2,3},{4,5},{6,7},{8,9},{10,11},{12,13},{14,15},{16,17},{18,... | collective-permute-start | bytes 442376 | tf_op jit(solution)/shard_map/ppermute | solution.py:318
  10.0 12.9 %collective-permute-start.5 = (bf16[144,512]{1,0:T(8,128)(2,1)S(1)}, bf16[144,512]{1,0:T(8,128)(2,1)S(1)}, u32[]{:S(2)}, u32[]{:S(2)}) collective-permute-start(bf16[144,512]{1,0:T(8,128)(2,1)S(1)} %collective-permute-done.4.refs_1_.refs_4_), channel_id=1, source_target_pairs={{2,3},{3,2},{6,7},{7,6},{10,11},{11,10},{14,15},{15,14},{18,19},{1... | collective-permute-start | bytes 442376 | tf_op jit(solution)/shard_map/ppermute | solution.py:321
  10.7 9.2 %collective-permute-start = (bf16[128,512]{1,0:T(8,128)(2,1)S(1)}, bf16[128,512]{1,0:T(8,128)(2,1)S(1)}, u32[]{:S(2)}, u32[]{:S(2)}) collective-permute-start(bf16[128,512]{1,0:T(8,128)(2,1)S(1)} %get-tuple-element.21), channel_id=1, source_target_pairs={{0,1},{1,0},{2,3},{4,5},{5,4},{6,7},{8,9},{9,8},{10,11},{12,13},{1... | collective-permute-start | bytes 393224 | tf_op jit(solution)/shard_map/ppermute | solution.py:318
  13.7 16.5 %collective-permute-start.1 = (bf16[128,512]{1,0:T(8,128)(2,1)S(1)}, bf16[128,512]{1,0:T(8,128)(2,1)S(1)}, u32[]{:S(2)}, u32[]{:S(2)}) collective-permute-start(bf16[128,512]{1,0:T(8,128)(2,1)S(1)} %get-tuple-element.21), channel_id=1, source_target_pairs={{0,2},{1,3},{4,6},{5,7},{8,10},{9,11},{12,14},{13,15},{16,18},{17,... | collective-permute-start | bytes 393224 | tf_op jit(solution)/shard_map/ppermute | solution.py:319
  19.9 10.3 %collective-permute-start.2 = (bf16[128,512]{1,0:T(8,128)(2,1)S(1)}, bf16[128,512]{1,0:T(8,128)(2,1)S(1)}, u32[]{:S(2)}, u32[]{:S(2)}) collective-permute-start(bf16[128,512]{1,0:T(8,128)(2,1)S(1)} %collective-permute-done.refs_0_), channel_id=1, source_target_pairs={{0,2},{1,3},{4,6},{5,7},{8,10},{9,11},{12,14},{13,15},{16,18},{17,... | collective-permute-start | bytes 393224 | tf_op jit(solution)/shard_map/ppermute | solution.py:321
  37.6 20.3 %collective-permute-start.6 = (bf16[128,1024]{1,0:T(8,128)(2,1)S(1)}, bf16[128,1024]{1,0:T(8,128)(2,1)S(1)}, u32[]{:S(2)}, u32[]{:S(2)}) collective-permute-start(bf16[128,1024]{1,0:T(8,128)(2,1)S(1)} %get-tuple-element.31), channel_id=1, source_target_pairs={{1,0},{3,2},{5,4},{7,6},{9,8},{11,10},{13,12},{15,14},{17,16},{19,... | collective-permute-start | bytes 786440 | tf_op jit(solution)/shard_map/ppermute | solution.py:443
  38.9 19.0 %collective-permute-start.7 = (bf16[128,1024]{1,0:T(8,128)(2,1)S(1)}, bf16[128,1024]{1,0:T(8,128)(2,1)S(1)}, u32[]{:S(2)}, u32[]{:S(2)}) collective-permute-start(bf16[128,1024]{1,0:T(8,128)(2,1)S(1)} %get-tuple-element.32), channel_id=1, source_target_pairs={{2,0},{3,1},{6,4},{7,5},{10,8},{11,9},{14,12},{15,13},{18,16},{19,... | collective-permute-start | bytes 786440 | tf_op jit(solution)/shard_map/ppermute | solution.py:443
  40.2 17.7 %collective-permute-start.8 = (bf16[128,1024]{1,0:T(8,128)(2,1)S(1)}, bf16[128,1024]{1,0:T(8,128)(2,1)S(1)}, u32[]{:S(2)}, u32[]{:S(2)}) collective-permute-start(bf16[128,1024]{1,0:T(8,128)(2,1)S(1)} %get-tuple-element.33), channel_id=1, source_target_pairs={{2,1},{3,0},{6,5},{7,4},{10,9},{11,8},{14,13},{15,12},{18,17},{19,... | collective-permute-start | bytes 786440 | tf_op jit(solution)/shard_map/ppermute | solution.py:443
